TPU v7x, 256 devices: a whole 4x4x8 slice. The times are simulated.
256 devices in a mesh: stripe: 16 (over y, x_hi, core), dev: 16 (over z, x_lo).
Axes of the slice: x: 4 (x_hi: 2, x_lo: 2; x = x_hi * 2 + x_lo), y: 4, z: 8, core: 2. Of those that a mesh axis runs over, the one named last changes fastest.
Arguments:
- row_factors: float32 [16384, 128], P(('stripe', 'dev')), may hold values from -1.8 to 1.8
- col_factors: float32 [262144, 128], P(('stripe', 'dev')), may hold values from -1.8 to 1.8
- ratings: bfloat16 [3, 8192, 128, 128], P(None, ('stripe', 'dev')), may hold values from -6 to 6
- rating_mask: int32 [3, 8192, 128, 128], P(None, ('stripe', 'dev')), may hold values 0 or 1
- tile_rows: int32 [3, 8192], P(None, ('stripe', 'dev')), may hold values from 0 to 7
- tile_cols: int32 [3, 8192], P(None, ('stripe', 'dev')), may hold values from 0 to 7
- tile_count: int32 [3, 256], P(None, ('stripe', 'dev')), may hold values from 1 to 32, as said below
Outputs:
- row_out: float32 [16384, 128], P(('stripe', 'dev'))
- col_out: float32 [262144, 128], P(('stripe', 'dev'))
Inputs may be any that keep to these rules, and one draw needn't show every extreme that they name: `tile_count`: slots past a device's count are padding. In every stratum some device has all 32 slots live.
All inputs are finite; a program needn't handle non-finite values. No bound on the sum of `rating_mask` on one device may be relied on, other than what follows from the above.
Results may differ from a plain program's by a relative error of at most 0.0003.
Values may be sent and summed in bfloat16 or wider, within the bound.
A program may use at most 128 MiB of HBM per device.

v0:
```python
import jax
import jax.numpy as jnp
from jax import lax
from jax.sharding import PartitionSpec as P

STRATA = 3


learn_rate = 0.02
ridge_weight = 2.5


def from_behind(value, axis, steps):
    count = lax.axis_size(axis)
    pairs = [(source, (source + steps) % count) for source in range(count)]
    return lax.ppermute(value, axis, pairs)


def tile_terms(stripe_rows, held_block, rating_tiles, mask_tiles, row_index, col_index, live_flags):
    tile_size = rating_tiles.shape[-1]
    rank_width = held_block.shape[1]
    row_blocks = stripe_rows.reshape(-1, tile_size, rank_width)
    col_blocks = held_block.reshape(-1, tile_size, rank_width)
    left_tiles = jnp.take(row_blocks, row_index, axis=0)
    right_tiles = jnp.take(col_blocks, col_index, axis=0)
    predicted = jnp.einsum("nik,njk->nij", left_tiles, right_tiles, precision=lax.Precision.HIGHEST)
    keep_entry = jnp.logical_and(mask_tiles > 0, live_flags[:, None, None])
    residual = jnp.where(keep_entry, predicted - rating_tiles.astype(jnp.float32), jnp.float32(0.0))
    row_grad = jnp.einsum("nij,njk->nik", residual, right_tiles, precision=lax.Precision.HIGHEST)
    col_grad = jnp.einsum("nij,nik->njk", residual, left_tiles, precision=lax.Precision.HIGHEST)
    row_onehot = (
        row_index[:, None] == jnp.arange(row_blocks.shape[0], dtype=jnp.int32)[None, :]
    ).astype(jnp.float32)
    col_onehot = (
        col_index[:, None] == jnp.arange(col_blocks.shape[0], dtype=jnp.int32)[None, :]
    ).astype(jnp.float32)
    grad_rows = jnp.einsum("nr,nik->rik", row_onehot, row_grad, precision=lax.Precision.HIGHEST)
    grad_cols = jnp.einsum("nc,njk->cjk", col_onehot, col_grad, precision=lax.Precision.HIGHEST)
    return (grad_rows.reshape(stripe_rows.shape), grad_cols.reshape(held_block.shape))


def shards(row_factors, col_factors, ratings, rating_mask, tile_rows, tile_cols, tile_count):
    shrink = 1.0 - learn_rate * ridge_weight
    slot_total = ratings.shape[1]
    held_block = col_factors
    own_rows = row_factors
    work_lists = [(ratings[0], rating_mask[0], tile_rows[0], tile_cols[0], tile_count[0])]
    for stratum in range(1, STRATA):
        work_lists.append(
            (
                ratings[stratum],
                rating_mask[stratum],
                tile_rows[stratum],
                tile_cols[stratum],
                tile_count[stratum],
            )
        )
    for stratum in range(STRATA):
        stripe_rows = lax.all_gather(own_rows, "dev", axis=0, tiled=True)
        rating_now, mask_now, rows_now, cols_now, count_now = work_lists[stratum]
        live_count = count_now[0]
        live_flags = jnp.arange(slot_total, dtype=jnp.int32) < live_count
        grad_rows, grad_cols = tile_terms(
            stripe_rows, held_block, rating_now, mask_now, rows_now, cols_now, live_flags
        )
        own_grad = lax.psum_scatter(grad_rows, "dev", scatter_dimension=0, tiled=True)
        own_rows = shrink * own_rows - learn_rate * own_grad
        held_block = shrink * held_block - learn_rate * grad_cols
        held_block = from_behind(held_block, "stripe", 1)
    return (own_rows, held_block)


def solution(mesh):
    in_specs = (
        P(("stripe", "dev"), None),
        P(("stripe", "dev"), None),
        P(None, ("stripe", "dev"), None, None),
        P(None, ("stripe", "dev"), None, None),
        P(None, ("stripe", "dev")),
        P(None, ("stripe", "dev")),
        P(None, ("stripe", "dev")),
    )
    out_specs = (P(("stripe", "dev"), None), P(("stripe", "dev"), None))
    return jax.shard_map(shards, mesh=mesh, in_specs=in_specs, out_specs=out_specs, check_vma=False)
```

profile of v0, /device:TPU:8, one launch (start us, length us, event | category | flops | bytes accessed | tf_op | source)
XLA Modules:
  0.0 400.5 jit_solution(13073664359849028182)
XLA Ops:
  7.2 0.0 reduce-scatter.4.cloned.1.call-start
  7.2 0.8 slice_bitcast_fusion.1
  8.0 0.8 compare_and_fusion
  8.8 39.3 %all_gather.9 = f32[1024,128]{1,0:T(8,128)S(1)} all-gather(f32[64,128]{1,0:T(8,128)} %param.9), channel_id=1, replica_groups=mesh['stripe'=16,'dev'=16] {'dev'}, dimensions={0}, use_global_device_ids=true | all-gather | bytes 557056 | tf_op jit(solution)/shard_map/all_gather | solution.py:59
  48.2 1.4 fusion.147
  49.6 0.6 iota_compare_fusion.8
  50.3 0.0 copy-start.3
  50.3 2.0 gather_fusion
  52.3 0.0 copy-done.3
  52.3 2.0 gather_fusion.1
  54.3 6.9 %fusion.44 = f32[32,128,128]{2,1,0:T(8,128)S(1)} fusion(f32[32,128,128]{2,1,0:T(8,128)} %gather_fusion.1, f32[32,128,128]{2,1,0:T(8,128)} %gather_fusion, pred[32]{0:T(512)(128)(4,1)S(1)} %get-tuple-element.27, pred[32]{0:T(512)(128)(4,1)S(1)} %get-tuple-element.32), kind=kOutput, calls=%fused_computation.50 | convolution fusion | flops 806354944 | bytes 6291520 | tf_op jit(solution)/shard_map/nik,njk->nij/dot_general | solution.py:26
  61.2 0.0 copy-done.2
  61.2 4.6 %fusion.23 = f32[32,128,128]{2,1,0:T(8,128)S(1)} fusion(f32[32,128,128]{2,1,0:T(8,128)S(1)} %fusion.44, s32[3,32,128,128]{3,2,1,0:T(8,128)} %param.12, f32[32,128,128]{2,1,0:T(8,128)S(1)} %copy-done.2, pred[32]{0:T(512)(128)(4,1)S(1)} %get-tuple-element.27, pred[32]{0:T(512)(128)(4,1)S(1)} %iota_compare_fusion.8, bf16[3,32,128,128]{3,2,1,0:T(8,128)(2,1)} %param.11), kind=kOutput, calls=%fused_computation.34 | convolution fusion | flops 808452096 | bytes 9437248 | tf_op jit(solution)/shard_map/nij,njk->nik/dot_general | solution.py:29
  65.8 2.0 fusion.13
  67.8 0.9 copy.9
  68.7 0.0 reduce-scatter.4.cloned.1.call-update
  68.7 0.0 copy-start.8
  68.7 0.6 reduce-scatter.6.cloned.1.call-start
  69.3 6.5 %fusion.21 = f32[32,128,128]{2,1,0:T(8,128)S(1)} fusion(f32[32,128,128]{2,1,0:T(8,128)S(1)} %fusion.44, s32[3,32,128,128]{3,2,1,0:T(8,128)} %param.12, f32[32,128,128]{2,1,0:T(8,128)} %gather_fusion, pred[32]{0:T(512)(128)(4,1)S(1)} %get-tuple-element.32, pred[32]{0:T(512)(128)(4,1)S(1)} %iota_compare_fusion.8, bf16[3,32,128,128]{3,2,1,0:T(8,128)(2,1)} %param.11), kind=kOutput, calls=%fused_computation.33 | convolution fusion | flops 808452096 | bytes 9437248 | tf_op jit(solution)/shard_map/nij,nik->njk/dot_general | solution.py:30
  75.8 2.0 fusion.48
  77.8 0.1 copy.10
  77.9 0.1 bitcast_subtract_fusion.2
  78.0 0.1 collective-permute-start
  78.1 0.7 iota_compare_fusion.7
  78.8 11.7 %collective-permute-done = f32[1024,128]{1,0:T(8,128)S(1)} collective-permute-done((f32[1024,128]{1,0:T(8,128)S(1)}, f32[1024,128]{1,0:T(8,128)S(1)}, u32[]{:S(2)}, u32[]{:S(2)}) %collective-permute-start) | collective-permute-done | bytes 524320 | tf_op jit(solution)/shard_map/ppermute | solution.py:16
  90.5 0.7 gather_fusion.3
  91.2 45.6 %reduce-scatter.4.cloned.1.call-done = f32[64,128]{1,0:T(8,128)} async-done(((f32[1024,128]{1,0:T(8,128)}), f32[64,128]{1,0:T(8,128)}) %reduce-scatter.4.cloned.1.call-update) | async-done | bytes 32784 | tf_op jit(solution)/shard_map/reduce_scatter | solution.py:66
  136.8 0.8 multiply_subtract_fusion.2
  137.5 33.3 %all_gather.10 = f32[1024,128]{1,0:T(8,128)S(1)} all-gather(f32[64,128]{1,0:T(8,128)S(1)} %multiply_subtract_fusion.2), channel_id=1, replica_groups=mesh['stripe'=16,'dev'=16] {'dev'}, dimensions={0}, use_global_device_ids=true | all-gather | bytes 557056 | tf_op jit(solution)/shard_map/all_gather | solution.py:59
  170.9 2.0 gather_fusion.2
  172.9 6.3 %fusion.39 = f32[32,128,128]{2,1,0:T(8,128)S(1)} fusion(f32[32,128,128]{2,1,0:T(8,128)S(1)} %gather_fusion.3, f32[32,128,128]{2,1,0:T(8,128)} %gather_fusion.2, pred[32]{0:T(512)(128)(4,1)S(1)} %get-tuple-element.25, pred[32]{0:T(512)(128)(4,1)S(1)} %get-tuple-element.34), kind=kOutput, calls=%fused_computation.45 | convolution fusion | flops 806354944 | bytes 6291520 | tf_op jit(solution)/shard_map/nik,njk->nij/dot_general | solution.py:26
  179.2 4.5 %fusion.27 = f32[32,128,128]{2,1,0:T(8,128)S(1)} fusion(f32[32,128,128]{2,1,0:T(8,128)S(1)} %fusion.39, s32[3,32,128,128]{3,2,1,0:T(8,128)} %param.12, f32[32,128,128]{2,1,0:T(8,128)S(1)} %gather_fusion.3, pred[32]{0:T(512)(128)(4,1)S(1)} %get-tuple-element.25, pred[32]{0:T(512)(128)(4,1)S(1)} %iota_compare_fusion.7, bf16[3,32,128,128]{3,2,1,0:T(8,128)(2,1)S(1)} %copy-done.4), kind=kOutput, calls=%fused_computation.36 | convolution fusion | flops 808452096 | bytes 9438208 | tf_op jit(solution)/shard_map/nij,njk->nik/dot_general | solution.py:29
  183.7 5.5 %fusion.25 = f32[32,128,128]{2,1,0:T(8,128)S(1)} fusion(f32[32,128,128]{2,1,0:T(8,128)S(1)} %fusion.39, s32[3,32,128,128]{3,2,1,0:T(8,128)} %param.12, f32[32,128,128]{2,1,0:T(8,128)S(1)} %copy-done, pred[32]{0:T(512)(128)(4,1)S(1)} %get-tuple-element.34, pred[32]{0:T(512)(128)(4,1)S(1)} %iota_compare_fusion.7, bf16[3,32,128,128]{3,2,1,0:T(8,128)(2,1)S(1)} %copy-done.4), kind=kOutput, calls=%fused_computation.35 | convolution fusion | flops 808452096 | bytes 9438208 | tf_op jit(solution)/shard_map/nij,nik->njk/dot_general | solution.py:30
  189.3 2.2 fusion.9
  191.4 0.9 copy.11
  192.3 0.0 reduce-scatter.6.cloned.1.call-update
  192.4 0.0 reduce-scatter.8.cloned.1.call-start
  192.4 2.0 fusion.51
  194.4 0.1 copy.12
  194.5 0.1 bitcast_subtract_fusion.1
  194.6 0.1 collective-permute-start.1
  194.7 0.7 iota_compare_fusion.6
  195.3 10.3 %collective-permute-done.1 = f32[1024,128]{1,0:T(8,128)S(1)} collective-permute-done((f32[1024,128]{1,0:T(8,128)S(1)}, f32[1024,128]{1,0:T(8,128)S(1)}, u32[]{:S(2)}, u32[]{:S(2)}) %collective-permute-start.1) | collective-permute-done | bytes 524320 | tf_op jit(solution)/shard_map/ppermute | solution.py:16
  205.7 0.7 gather_fusion.5
  206.3 57.4 %reduce-scatter.6.cloned.1.call-done = f32[64,128]{1,0:T(8,128)} async-done(((f32[1024,128]{1,0:T(8,128)}), f32[64,128]{1,0:T(8,128)}) %reduce-scatter.6.cloned.1.call-update) | async-done | bytes 32784 | tf_op jit(solution)/shard_map/reduce_scatter | solution.py:66
  263.7 0.8 multiply_subtract_fusion.1
  264.5 33.0 %all_gather.11 = f32[1024,128]{1,0:T(8,128)S(1)} all-gather(f32[64,128]{1,0:T(8,128)S(1)} %multiply_subtract_fusion.1), channel_id=1, replica_groups=mesh['stripe'=16,'dev'=16] {'dev'}, dimensions={0}, use_global_device_ids=true | all-gather | bytes 557056 | tf_op jit(solution)/shard_map/all_gather | solution.py:59
  297.5 2.0 gather_fusion.4
  299.5 6.3 %fusion.34 = f32[32,128,128]{2,1,0:T(8,128)S(1)} fusion(f32[32,128,128]{2,1,0:T(8,128)S(1)} %gather_fusion.5, f32[32,128,128]{2,1,0:T(8,128)} %gather_fusion.4, pred[32]{0:T(512)(128)(4,1)S(1)} %get-tuple-element.5, pred[32]{0:T(512)(128)(4,1)S(1)} %get-tuple-element.36), kind=kOutput, calls=%fused_computation.40 | convolution fusion | flops 806354944 | bytes 6291520 | tf_op jit(solution)/shard_map/nik,njk->nij/dot_general | solution.py:26
  305.8 6.9 %fusion.29 = f32[32,128,128]{2,1,0:T(8,128)} fusion(f32[32,128,128]{2,1,0:T(8,128)S(1)} %fusion.34, s32[3,32,128,128]{3,2,1,0:T(8,128)} %param.12, f32[32,128,128]{2,1,0:T(8,128)S(1)} %copy-done.1, pred[32]{0:T(512)(128)(4,1)S(1)} %get-tuple-element.36, pred[32]{0:T(512)(128)(4,1)S(1)} %iota_compare_fusion.6, bf16[3,32,128,128]{3,2,1,0:T(8,128)(2,1)S(1)} %copy-done.5), kind=kOutput, calls=%fused_computation.37 | convolution fusion | flops 808452096 | bytes 9438208 | tf_op jit(solution)/shard_map/nij,nik->njk/dot_general | solution.py:30
  312.7 4.4 %fusion.31 = f32[32,128,128]{2,1,0:T(8,128)S(1)} fusion(f32[32,128,128]{2,1,0:T(8,128)S(1)} %fusion.34, s32[3,32,128,128]{3,2,1,0:T(8,128)} %param.12, f32[32,128,128]{2,1,0:T(8,128)S(1)} %gather_fusion.5, pred[32]{0:T(512)(128)(4,1)S(1)} %get-tuple-element.5, pred[32]{0:T(512)(128)(4,1)S(1)} %iota_compare_fusion.6, bf16[3,32,128,128]{3,2,1,0:T(8,128)(2,1)S(1)} %copy-done.5), kind=kOutput, calls=%fused_computation.38 | convolution fusion | flops 808452096 | bytes 9438208 | tf_op jit(solution)/shard_map/nij,njk->nik/dot_general | solution.py:29
  317.1 0.0 copy-start.6
  317.1 2.2 fusion.5
  319.3 0.9 copy.13
  320.2 0.0 reduce-scatter.8.cloned.1.call-update
  320.2 0.0 copy-done.6
  320.2 2.0 fusion.54
  322.2 0.1 copy.14
  322.3 0.1 bitcast_subtract_fusion
  322.4 0.1 collective-permute-start.2
  322.5 11.0 %collective-permute-done.2 = f32[1024,128]{1,0:T(8,128)S(1)} collective-permute-done((f32[1024,128]{1,0:T(8,128)S(1)}, f32[1024,128]{1,0:T(8,128)S(1)}, u32[]{:S(2)}, u32[]{:S(2)}) %collective-permute-start.2) | collective-permute-done | bytes 524320 | tf_op jit(solution)/shard_map/ppermute | solution.py:16
  333.5 57.9 %reduce-scatter.8.cloned.1.call-done = f32[64,128]{1,0:T(8,128)} async-done(((f32[1024,128]{1,0:T(8,128)}), f32[64,128]{1,0:T(8,128)}) %reduce-scatter.8.cloned.1.call-update) | async-done | bytes 32784 | tf_op jit(solution)/shard_map/reduce_scatter | solution.py:66
  391.4 1.4 multiply_subtract_fusion
  392.7 0.8 copy.40
  (19 shorter events, 0.1 us)
Async XLA Ops:
  7.2 129.6 %reduce-scatter.4.cloned.1.call-start = ((), (), s32[]{:S(2)}) async-start(), calls=%async_computation.3 | async-start | bytes 557056 | tf_op jit(solution)/shard_map/reduce_scatter | solution.py:66
  50.3 2.0 copy-start.3
  54.3 6.9 %copy-start.2 = (f32[32,128,128]{2,1,0:T(8,128)S(1)}, f32[32,128,128]{2,1,0:T(8,128)}, u32[]{:S(2)}) copy-start(f32[32,128,128]{2,1,0:T(8,128)} %gather_fusion.1) | copy-start | bytes 6291460
  68.7 7.1 %copy-start.8 = (s32[3,32]{1,0:T(4,128)S(1)}, s32[3,32]{1,0:T(4,128)}, u32[]{:S(2)}) copy-start(s32[3,32]{1,0:T(4,128)} %param.14) | copy-start | bytes 1156
  68.7 195.0 %reduce-scatter.6.cloned.1.call-start = ((), (), s32[]{:S(2)}) async-start(), calls=%async_computation.4 | async-start | bytes 557056 | tf_op jit(solution)/shard_map/reduce_scatter | solution.py:66
  78.0 12.5 %collective-permute-start = (f32[1024,128]{1,0:T(8,128)S(1)}, f32[1024,128]{1,0:T(8,128)S(1)}, u32[]{:S(2)}, u32[]{:S(2)}) collective-permute-start(f32[1024,128]{1,0:T(8,128)S(1)} %bitcast_subtract_fusion.2), channel_id=1, source_target_pairs={{0,16},{16,32},{32,48},{48,64},{64,80},{80,96},{96,112},{112,128},... | collective-permute-start | bytes 1572872 | tf_op jit(solution)/shard_map/ppermute | solution.py:16
  90.5 46.3 %copy-start.7 = (f32[64,128]{1,0:T(8,128)S(1)}, f32[64,128]{1,0:T(8,128)}, u32[]{:S(2)}) copy-start(f32[64,128]{1,0:T(8,128)} %param.9) | copy-start | bytes 98308
  172.9 6.3 %copy-start.4 = (bf16[3,32,128,128]{3,2,1,0:T(8,128)(2,1)S(1)}, bf16[3,32,128,128]{3,2,1,0:T(8,128)(2,1)}, u32[]{:S(2)}) copy-start(bf16[3,32,128,128]{3,2,1,0:T(8,128)(2,1)} %param.11) | copy-start | bytes 9437188
  179.2 4.5 %copy-start = (f32[32,128,128]{2,1,0:T(8,128)S(1)}, f32[32,128,128]{2,1,0:T(8,128)}, u32[]{:S(2)}) copy-start(f32[32,128,128]{2,1,0:T(8,128)} %gather_fusion.2) | copy-start | bytes 6291460
  192.4 199.0 %reduce-scatter.8.cloned.1.call-start = ((), (), s32[]{:S(2)}) async-start(), calls=%async_computation.5 | async-start | bytes 557056 | tf_op jit(solution)/shard_map/reduce_scatter | solution.py:66
  194.6 11.1 %collective-permute-start.1 = (f32[1024,128]{1,0:T(8,128)S(1)}, f32[1024,128]{1,0:T(8,128)S(1)}, u32[]{:S(2)}, u32[]{:S(2)}) collective-permute-start(f32[1024,128]{1,0:T(8,128)S(1)} %bitcast_subtract_fusion.1), channel_id=1, source_target_pairs={{0,16},{16,32},{32,48},{48,64},{64,80},{80,96},{96,112},{112,128},... | collective-permute-start | bytes 1572872 | tf_op jit(solution)/shard_map/ppermute | solution.py:16
  299.5 6.3 %copy-start.1 = (f32[32,128,128]{2,1,0:T(8,128)S(1)}, f32[32,128,128]{2,1,0:T(8,128)}, u32[]{:S(2)}) copy-start(f32[32,128,128]{2,1,0:T(8,128)} %gather_fusion.4) | copy-start | bytes 6291460
  299.5 6.3 %copy-start.5 = (bf16[3,32,128,128]{3,2,1,0:T(8,128)(2,1)S(1)}, bf16[3,32,128,128]{3,2,1,0:T(8,128)(2,1)}, u32[]{:S(2)}) copy-start(bf16[3,32,128,128]{3,2,1,0:T(8,128)(2,1)} %param.11) | copy-start | bytes 9437188
  317.1 3.1 copy-start.6
  322.4 11.1 %collective-permute-start.2 = (f32[1024,128]{1,0:T(8,128)S(1)}, f32[1024,128]{1,0:T(8,128)S(1)}, u32[]{:S(2)}, u32[]{:S(2)}) collective-permute-start(f32[1024,128]{1,0:T(8,128)S(1)} %bitcast_subtract_fusion), channel_id=1, source_target_pairs={{0,16},{16,32},{32,48},{48,64},{64,80},{80,96},{96,112},{112,128},... | collective-permute-start | bytes 1572872 | tf_op jit(solution)/shard_map/ppermute | solution.py:16
Sparse Core Ops, SparseCore 0:
  68.8 67.8 reduce-scatter.3
  192.5 71.1 reduce-scatter.5
  320.3 70.9 reduce-scatter.7
where the time goes:
time: 408 us; the launch traced here: 401 us
  waiting for transfers between devices  194 us (48%)
  blocking collectives  106 us (26%)
  matrix products  64.1 us (16%)
  local copies, waits for them, and re-layouts  15.5 us (4%)
  between operations  14.5 us (4%)
  other arithmetic  5.96 us (1%)
    reduce_scatter x3, waiting for transfers between devices, shards(): lax.psum_scatter(grad_rows, 'dev', scatter_dimension=0, tiled=True)  161 us
    all_gather x3, blocking collectives, shards(): stripe_rows = lax.all_gather(own_rows, 'dev', axis=0, tiled=True)  106 us
    ppermute x3, waiting for transfers between devices, from_behind(): return lax.ppermute(value, axis, pairs)  33 us
    dot_general x3, matrix products, tile_terms(): jnp.einsum('nik,njk->nij', left_tiles, right_tiles, precision=lax.Precisi...  19.5 us
    dot_general x3, matrix products, tile_terms(): jnp.einsum('nij,nik->njk', residual, left_tiles, precision=lax.Precision....  18.9 us
    dot_general x3, matrix products, tile_terms(): jnp.einsum('nij,njk->nik', residual, right_tiles, precision=lax.Precision...  13.5 us
  transfers between devices with their start and end apart: 6, of which 6 were waited for; matrix products, arithmetic and copies ran while one was open for 4% of the time, Pallas kernels for 0%

commit v1 on v0

v1 whole, which is shorter than its diff:
```python
import functools

import jax
import jax.numpy as jnp
from jax import lax
from jax.experimental import pallas as pl
from jax.experimental.pallas import tpu as pltpu
from jax.sharding import PartitionSpec as P

MESH = pl.DeviceIdType.MESH
STRATA = 3
LEARN_RATE = 0.02
RIDGE_WEIGHT = 2.5
SHRINK = 1.0 - LEARN_RATE * RIDGE_WEIGHT
F32, BF16, I16 = jnp.float32, jnp.bfloat16, jnp.int16
TOP = 32767.0
NT = (((1,), (1,)), ((), ()))
NN = (((1,), (0,)), ((), ()))
TN = (((0,), (0,)), ((), ()))


def mm(a, b, dims):
    return lax.dot_general(a, b, dims, preferred_element_type=F32)


def split(x):
    hi = x.astype(BF16)
    return hi, (x - hi.astype(F32)).astype(BF16)


def quantize(x):
    peak = jnp.maximum(jnp.max(jnp.abs(x), axis=0, keepdims=True), 1e-30)
    code = jnp.round(x * (TOP / peak)).astype(jnp.int32).astype(I16)
    return code, peak * (1.0 / TOP)


def decode(code, scale):
    return code.astype(jnp.int32).astype(F32) * scale


def kernel(
    n_stripe, n_dev, order_s, start_s, own_ref, h0_ref, rat_ref, mask_ref, uout_ref, hout_ref,
    rat_a, rat_b, rat_c, mask_a, mask_b, mask_c, psm, psr, u2, hhh, hcat, e_hi, e_lo, hbuf, own, g_tile, g_own,
    rs_src, rs_src_sc, rs_dst, rs_dst_sc, ag_src, ag_src_sc, ag_dst, ag_dst_sc,
    in_sem, rs_ss, rs_rs, rs_ss2, rs_rs2, ag_ss, ag_rs, ag_ss2, ag_rs2, h_ss, h_rs,
):
    s, d = lax.axis_index("stripe"), lax.axis_index("dev")
    z, lo = d // 2, d % 2
    ahead = (s + 1) % n_stripe
    behind = (s + n_stripe - 1) % n_stripe

    barrier = pltpu.get_barrier_semaphore()
    for k in range(1, n_dev):
        pl.semaphore_signal(barrier, inc=1, device_id=(s, (d + k) % n_dev), device_id_type=MESH)
    for other in (ahead, behind):
        pl.semaphore_signal(barrier, inc=1, device_id=(other, d), device_id_type=MESH)

    rat_v, mask_v = (rat_a, rat_b, rat_c), (mask_a, mask_b, mask_c)
    loads = []
    for t in range(STRATA):
        loads.append((
            pltpu.make_async_copy(rat_ref.at[t], rat_v[t], in_sem.at[2 * t]),
            pltpu.make_async_copy(mask_ref.at[t], mask_v[t], in_sem.at[2 * t + 1]),
        ))
        for load in loads[t]:
            load.start()

    def set_u(rows, x):
        hi, low = split(x)
        u2[rows, 0:128] = hi
        u2[rows, 128:256] = low

    def set_h(source):
        def body(c, carry):
            rows = pl.ds(pl.multiple_of(c * 128, 128), 128)
            hi, low = split(source[rows, :])
            hhh[rows, 0:128] = hi
            hhh[rows, 128:256] = hi
            hcat[rows, 0:128] = hi
            hcat[rows, 128:256] = low
            return carry

        lax.fori_loop(0, 8, body, 0)

    def prefix(t):
        for load in loads[t]:
            load.wait()

        def body(i, carry):
            slot = order_s[t, i]
            seen = mask_v[t][slot] > 0
            value = jnp.where(seen, rat_v[t][slot].astype(F32), 0.0)
            psm[i + 1] = psm[i] + jnp.where(seen, 1.0, 0.0)
            psr[i + 1] = psr[i] + value
            return carry

        lax.fori_loop(0, 32, body, 0)

    def rs_copy(j):
        return (
            pltpu.make_async_remote_copy(
                src_ref=rs_src.at[j], dst_ref=rs_dst.at[d], send_sem=rs_ss.at[j], recv_sem=rs_rs.at[d],
                device_id=(s, j), device_id_type=MESH),
            pltpu.make_async_remote_copy(
                src_ref=rs_src_sc.at[j], dst_ref=rs_dst_sc.at[d], send_sem=rs_ss2.at[j], recv_sem=rs_rs2.at[d],
                device_id=(s, j), device_id_type=MESH),
        )

    def rs_arrival(j):
        return (
            pltpu.make_async_remote_copy(
                src_ref=rs_src.at[j], dst_ref=rs_dst.at[j], send_sem=rs_ss.at[j], recv_sem=rs_rs.at[j],
                device_id=(s, j), device_id_type=MESH),
            pltpu.make_async_remote_copy(
                src_ref=rs_src_sc.at[j], dst_ref=rs_dst_sc.at[j], send_sem=rs_ss2.at[j], recv_sem=rs_rs2.at[j],
                device_id=(s, j), device_id_type=MESH),
        )

    def ag_copy(j):
        return (
            pltpu.make_async_remote_copy(
                src_ref=ag_src, dst_ref=ag_dst.at[d], send_sem=ag_ss.at[j], recv_sem=ag_rs.at[d],
                device_id=(s, j), device_id_type=MESH),
            pltpu.make_async_remote_copy(
                src_ref=ag_src_sc, dst_ref=ag_dst_sc.at[d], send_sem=ag_ss2.at[j], recv_sem=ag_rs2.at[d],
                device_id=(s, j), device_id_type=MESH),
        )

    def ag_arrival(j):
        return (
            pltpu.make_async_remote_copy(
                src_ref=ag_src, dst_ref=ag_dst.at[j], send_sem=ag_ss.at[j], recv_sem=ag_rs.at[j],
                device_id=(s, j), device_id_type=MESH),
            pltpu.make_async_remote_copy(
                src_ref=ag_src_sc, dst_ref=ag_dst_sc.at[j], send_sem=ag_ss2.at[j], recv_sem=ag_rs2.at[j],
                device_id=(s, j), device_id_type=MESH),
        )

    def far_first(i):
        return 4 + (i // 2) - (i % 2) * (2 * (i // 2) + 1)

    def ag_send():
        for k in (8, 9, 7, 6, 10, 5, 11, 4, 12, 3, 13, 2, 14, 1, 15):
            j = (d + k) % n_dev
            for copy in ag_copy(j):
                copy.start()

    def ag_prepare():
        rows = pl.ds(pl.multiple_of(d * 64, 64), 64)
        code, scale = quantize(own[...])
        ag_src[...] = code
        ag_src_sc[...] = scale
        set_u(rows, own[...])

    def ag_take():
        def body(k, carry):
            j = (d + k) % n_dev
            for copy in ag_arrival(j):
                copy.wait_recv()
            set_u(pl.ds(pl.multiple_of(j * 64, 64), 64), decode(ag_dst[j], ag_dst_sc[j]))
            return carry

        lax.fori_loop(1, n_dev, body, 0)

        def drain(k, carry):
            for copy in ag_copy((d + k) % n_dev):
                copy.wait_send()
            return carry

        lax.fori_loop(1, n_dev, drain, 0)

    def row_tile(t, r):
        rows = pl.ds(pl.multiple_of(r * 128, 128), 128)
        u_both = u2[rows, :]
        u_hi = u2[rows, 0:128]
        for c in range(4):
            cols = slice(c * 256, (c + 1) * 256)
            pred = mm(u_both, hhh[cols, :], NT) + mm(u_hi, hcat[cols, 128:256], NT)
            for half in range(2):
                cell = r * 8 + c * 2 + half
                begin, end = start_s[t, cell], start_s[t, cell + 1]
                weight = psm[end] - psm[begin]
                total = psr[end] - psr[begin]
                err = weight * pred[:, half * 128:(half + 1) * 128] - total
                hi, low = split(err)
                at = slice(c * 256 + half * 128, c * 256 + half * 128 + 128)
                e_hi[rows, at] = hi
                e_lo[rows, at] = low
        both = mm(e_hi[rows, :], hcat[...], NN)
        return both[:, 0:128] + both[:, 128:256] + mm(e_lo[rows, :], hcat[:, 0:128], NN)

    def phase1(t):
        def body(i, carry):
            r = (z + far_first(i)) % 8
            g_tile[...] = row_tile(t, r)
            for half in range(2):
                j = 2 * r + half
                code, scale = quantize(g_tile[half * 64:(half + 1) * 64, :])
                rs_src[j] = code
                rs_src_sc[j] = scale
                for copy in rs_copy(j):
                    copy.start()
            return carry

        lax.fori_loop(0, 7, body, 0)
        g_tile[...] = row_tile(t, z)
        other = d + 1 - 2 * lo
        code, scale = quantize(g_tile[pl.ds(pl.multiple_of((1 - lo) * 64, 64), 64), :])
        rs_src[other] = code
        rs_src_sc[other] = scale
        for copy in rs_copy(other):
            copy.start()
        g_own[...] = g_tile[pl.ds(pl.multiple_of(lo * 64, 64), 64), :]

    def h_copy(t, c):
        rows = pl.ds(pl.multiple_of(c * 128, 128), 128)
        target = hbuf.at[t + 1, rows] if t + 1 < STRATA else hout_ref.at[rows]
        return pltpu.make_async_remote_copy(
            src_ref=hbuf.at[t, rows], dst_ref=target, send_sem=h_ss.at[8 * t + c], recv_sem=h_rs.at[8 * t + c],
            device_id=(ahead, d), device_id_type=MESH)

    def phase2(t):
        def body(c, carry):
            cols = pl.ds(pl.multiple_of(c * 128, 128), 128)
            both = mm(e_hi[:, cols], u2[...], TN)
            grad = both[:, 0:128] + both[:, 128:256] + mm(e_lo[:, cols], u2[:, 0:128], TN)
            old = h0_ref[cols, :] if t == 0 else hbuf[t, cols, :]
            hbuf[t, cols, :] = SHRINK * old - LEARN_RATE * grad
            h_copy(t, c).start()
            return carry

        lax.fori_loop(0, 8, body, 0)

    def rs_sum():
        def body(k, total):
            j = (d + k) % n_dev
            for copy in rs_arrival(j):
                copy.wait_recv()
            return total + decode(rs_dst[j], rs_dst_sc[j])

        total = lax.fori_loop(1, n_dev, body, g_own[...])
        own[...] = SHRINK * own[...] - LEARN_RATE * total

        def drain(k, carry):
            for copy in rs_copy((d + k) % n_dev):
                copy.wait_send()
            return carry

        lax.fori_loop(1, n_dev, drain, 0)

    own[...] = own_ref[...]
    psm[0] = jnp.zeros_like(psm[0])
    psr[0] = jnp.zeros_like(psr[0])
    ag_prepare()
    pl.semaphore_wait(barrier, n_dev + 1)
    ag_send()
    set_h(h0_ref)
    prefix(0)
    ag_take()
    for t in range(STRATA):
        phase1(t)
        phase2(t)
        if t + 1 < STRATA:
            prefix(t + 1)
        rs_sum()
        if t + 1 < STRATA:
            ag_prepare()
            ag_send()

            def landed(c, carry):
                h_copy(t, c).wait_recv()
                return carry

            lax.fori_loop(0, 8, landed, 0)
            set_h(hbuf.at[t + 1])
            ag_take()
    uout_ref[...] = own[...]

    def landed(c, carry):
        h_copy(STRATA - 1, c).wait_recv()
        return carry

    lax.fori_loop(0, 8, landed, 0)
    for t in range(STRATA):

        def sent(c, carry):
            h_copy(t, c).wait_send()
            return carry

        lax.fori_loop(0, 8, sent, 0)


def tile_lists(tile_rows, tile_cols, tile_count):
    slots = tile_rows.shape[1]
    index = jnp.arange(slots, dtype=jnp.int32)
    key = jnp.where(index[None, :] < tile_count, tile_rows * 8 + tile_cols, 64)
    unique = key * slots + index[None, :]
    rank = jnp.sum((unique[:, None, :] < unique[:, :, None]).astype(jnp.int32), axis=2)
    order = jnp.sum(jnp.where(rank[:, None, :] == index[None, :, None], index[None, None, :], 0), axis=2)
    cells = jnp.arange(72, dtype=jnp.int32)
    start = jnp.sum((key[:, None, :] < cells[None, :, None]).astype(jnp.int32), axis=2)
    return order, start


def shards(n_stripe, n_dev, row_factors, col_factors, ratings, rating_mask, tile_rows, tile_cols, tile_count):
    order, start = tile_lists(tile_rows, tile_cols, tile_count)
    vmem, smem, anywhere = (pl.BlockSpec(memory_space=m) for m in (pltpu.VMEM, pltpu.SMEM, pl.ANY))
    dma = lambda n: pltpu.SemaphoreType.DMA((n,))
    return pl.pallas_call(
        functools.partial(kernel, n_stripe, n_dev),
        out_shape=(
            jax.ShapeDtypeStruct(row_factors.shape, F32),
            jax.ShapeDtypeStruct(col_factors.shape, F32),
        ),
        in_specs=[smem, smem, vmem, vmem, anywhere, anywhere],
        out_specs=(vmem, anywhere),
        scratch_shapes=[
            *[pltpu.VMEM((32, 128, 128), BF16)] * 3,
            *[pltpu.VMEM((32, 128, 128), jnp.int32)] * 3,
            pltpu.VMEM((33, 128, 128), F32),
            pltpu.VMEM((33, 128, 128), F32),
            pltpu.VMEM((1024, 256), BF16),
            pltpu.VMEM((1024, 256), BF16),
            pltpu.VMEM((1024, 256), BF16),
            pltpu.VMEM((1024, 1024), BF16),
            pltpu.VMEM((1024, 1024), BF16),
            pltpu.VMEM((3, 1024, 128), F32),
            pltpu.VMEM((64, 128), F32),
            pltpu.VMEM((128, 128), F32),
            pltpu.VMEM((64, 128), F32),
            pltpu.VMEM((16, 64, 128), I16),
            pltpu.VMEM((16, 1, 128), F32),
            pltpu.VMEM((16, 64, 128), I16),
            pltpu.VMEM((16, 1, 128), F32),
            pltpu.VMEM((64, 128), I16),
            pltpu.VMEM((1, 128), F32),
            pltpu.VMEM((16, 64, 128), I16),
            pltpu.VMEM((16, 1, 128), F32),
            dma(6), dma(16), dma(16), dma(16), dma(16), dma(16), dma(16), dma(16), dma(16), dma(24), dma(24),
        ],
        compiler_params=pltpu.CompilerParams(
            collective_id=0, has_side_effects=True, vmem_limit_bytes=56 * 1024 * 1024
        ),
    )(order, start, row_factors, col_factors, ratings, rating_mask)


def solution(mesh):
    in_specs = (
        P(("stripe", "dev"), None),
        P(("stripe", "dev"), None),
        P(None, ("stripe", "dev"), None, None),
        P(None, ("stripe", "dev"), None, None),
        P(None, ("stripe", "dev")),
        P(None, ("stripe", "dev")),
        P(None, ("stripe", "dev")),
    )
    out_specs = (P(("stripe", "dev"), None), P(("stripe", "dev"), None))
    body = functools.partial(shards, mesh.shape["stripe"], mesh.shape["dev"])
    return jax.shard_map(body, mesh=mesh, in_specs=in_specs, out_specs=out_specs, check_vma=False)
```

time: 408 us -> 81 us (0.20); the launches traced: 401 us -> 80 us
  waiting for transfers between devices: 194 us -> 0 us
  blocking collectives: 106 us -> 0 us
  Pallas kernels: 0 us -> 73.7 us
  matrix products: 64.1 us -> 0 us
  between operations: 14.5 us -> 0.64 us
  local copies, waits for them, and re-layouts: 15.5 us -> 3.24 us
    reduce_scatter x3 -> x0, waiting for transfers between devices: 161 us -> none  [shards(): lax.psum_scatter(grad_rows, 'dev', scatter_dimension=0, tiled=True)]
    all_gather x3 -> x0, blocking collectives: 106 us -> none  [shards(): stripe_rows = lax.all_gather(own_rows, 'dev', axis=0, tiled=True)]
    pallas_call x0 -> x1, Pallas kernels: none -> 73.7 us  [shards(): pl.pallas_call(functools.partial(kernel, n_stripe, n_dev), out_shape=(jax...]
    dot_general x15 -> x0, matrix products: 64.1 us -> none  [the longest x3 19.5 us: tile_terms(): jnp.einsum('nik,njk->nij', left_tiles, right_tiles, precision=lax.Precisi...]
    ppermute x3 -> x0, waiting for transfers between devices: 33 us -> none  [from_behind(): return lax.ppermute(value, axis, pairs)]
    gather x6 -> x0, local copies, waits for them, and re-layouts: 9.4 us -> none  [the longest x3 6.03 us: tile_terms(): left_tiles = jnp.take(row_blocks, row_index, axis=0)]
  transfers between devices with their start and end apart: 6 -> 0, of which waited for: 6 -> 0; matrix products, arithmetic and copies ran while one was open for 4% -> 0% of each run, Pallas kernels for 0% -> 0%
where the time goes in v1:
time: 81 us; the launch traced here: 80 us
  Pallas kernels  73.7 us (91%)
  local copies, waits for them, and re-layouts  3.24 us (4%)
  other arithmetic  2.4 us (3%)
    pallas_call x1, Pallas kernels, shards(): pl.pallas_call(functools.partial(kernel, n_stripe, n_dev), out_shape=(jax...  73.7 us
    unnamed x2, local copies, waits for them, and re-layouts  3.24 us

profile of v1, /device:TPU:8, one launch (start us, length us, event | category | flops | bytes accessed | tf_op | source)
XLA Modules:
  0.0 80.0 jit_solution(907546938664448307)
XLA Ops:
  0.6 0.8 iota_add_fusion
  1.4 0.2 convert_reduce_fusion.1
  1.6 0.7 select_reduce_fusion.order_s
  2.4 0.7 convert_reduce_fusion.start_s
  3.0 73.7 %shard_map.86 = (f32[64,128]{1,0:T(8,128)}, f32[1024,128]{1,0:T(8,128)}) custom-call(s32[3,32]{1,0:T(4,128)} %select_reduce_fusion.order_s, s32[3,72]{1,0:T(4,128)} %convert_reduce_fusion.start_s, f32[64,128]{1,0:T(8,128)} %own_ref.1, f32[1024,128]{1,0:T(8,128)} %h0_ref.1, bf16[3,32,128,128]{3,2,1,0:T(8,128)(2,1)} %rat_ref.1, s32[3,32,128,128]{3,2,1,0:T(8,128)} %mask_ref.1), custom_call_target="tpu_custom_call" | custom-call | tf_op jit(solution)/shard_map/pallas_call | solution.py:309
  76.7 1.4 %copy.11 = f32[64,128]{1,0:T(8,128)} copy(f32[64,128]{1,0:T(8,128)} %get-tuple-element.6) | data formatting | bytes 65536
  78.1 1.9 %copy.12 = f32[1024,128]{1,0:T(8,128)} copy(f32[1024,128]{1,0:T(8,128)} %get-tuple-element.7) | data formatting | bytes 1048576

commit v2 on v0

v2 whole, which is shorter than its diff:
```python
import functools

import jax
import jax.numpy as jnp
from jax import lax
from jax.experimental import pallas as pl
from jax.experimental.pallas import tpu as pltpu
from jax.sharding import PartitionSpec as P

MESH = pl.DeviceIdType.MESH
STRATA = 3
LEARN_RATE = 0.02
RIDGE_WEIGHT = 2.5
SHRINK = 1.0 - LEARN_RATE * RIDGE_WEIGHT
F32, BF16, I16 = jnp.float32, jnp.bfloat16, jnp.int16
TOP = 32767.0
NT = (((1,), (1,)), ((), ()))
NN = (((1,), (0,)), ((), ()))
TN = (((0,), (0,)), ((), ()))


def mm(a, b, dims):
    return lax.dot_general(a, b, dims, preferred_element_type=F32)


def split(x):
    hi = x.astype(BF16)
    return hi, (x - hi.astype(F32)).astype(BF16)


def quantize(x):
    peak = jnp.maximum(jnp.max(jnp.abs(x), axis=0, keepdims=True), 1e-30)
    code = jnp.round(x * (TOP / peak)).astype(jnp.int32).astype(I16)
    return code, peak * (1.0 / TOP)


def decode(code, scale):
    return code.astype(jnp.int32).astype(F32) * scale


def kernel(
    n_stripe, n_dev, order_s, start_s, own_ref, h0_ref, rat_ref, mask_ref, uout_ref, code_ref, scale_ref,
    rat_v, mask_v, psm, psr, dm, dr, u3, h3, hcat, e_hi, e_lo, hcur, own, g_tile, g_own,
    rs_src, rs_src_sc, rs_dst, rs_dst_sc, ag_src, ag_src_sc, ag_dst, ag_dst_sc, h_src, h_src_sc, h_dst, h_dst_sc,
    in_sem, rs_ss, rs_rs, rs_ss2, rs_rs2, ag_ss, ag_rs, ag_ss2, ag_rs2, h_ss, h_rs, h_ss2, h_rs2,
):
    s, d = lax.axis_index("stripe"), lax.axis_index("dev")
    ahead = lax.rem(s + 1, n_stripe)
    behind = lax.rem(s + n_stripe - 1, n_stripe)
    far_first = (8, 9, 7, 6, 10, 5, 11, 4, 12, 3, 13, 2, 14, 1, 15)

    def peer(k):
        return lax.rem(d + k, n_dev)

    barrier = pltpu.get_barrier_semaphore()
    for k in range(1, n_dev):
        pl.semaphore_signal(barrier, inc=1, device_id=(s, peer(k)), device_id_type=MESH)
    for other in (ahead, behind):
        pl.semaphore_signal(barrier, inc=1, device_id=(other, d), device_id_type=MESH)

    def loads(t):
        return (
            pltpu.make_async_copy(rat_ref.at[t], rat_v, in_sem.at[0]),
            pltpu.make_async_copy(mask_ref.at[t], mask_v, in_sem.at[1]),
        )

    def load(t):
        for copy in loads(t):
            copy.start()

    def set_h(value, save):
        def body(c, carry):
            rows = pl.ds(pl.multiple_of(c * 128, 128), 128)
            x = value(c, rows)
            if save:
                hcur[rows, :] = x
            hi, low = split(x)
            hcat[rows, 0:128] = hi
            hcat[rows, 128:256] = low
            hi, low = split(x.T)
            h3[0:128, rows] = hi
            h3[128:256, rows] = hi
            h3[256:384, rows] = low
            return carry

        lax.fori_loop(0, 8, body, 0)

    def prefix(t):
        for copy in loads(t):
            copy.wait()

        def body(i, carry):
            slot = order_s[t, i]
            seen = mask_v[slot] > 0
            value = jnp.where(seen, rat_v[slot].astype(F32), 0.0)
            psm[i + 1] = psm[i] + jnp.where(seen, 1.0, 0.0)
            psr[i + 1] = psr[i] + value
            return carry

        lax.fori_loop(0, 32, body, 0)

    def dense(t):
        def body(r, carry):
            for c in range(8):
                begin, end = start_s[t, r * 8 + c], start_s[t, r * 8 + c + 1]
                weight = psm[end] - psm[begin]
                total = psr[end] - psr[begin]
                for b in range(2):
                    for f in range(2):
                        rows = slice(b * 64 + f * 32, b * 64 + f * 32 + 32)
                        at = pl.ds(pl.multiple_of(f * 512 + r * 64 + b * 32, 32), 32)
                        dm[at, c * 128:(c + 1) * 128] = weight[rows, :]
                        dr[at, c * 128:(c + 1) * 128] = total[rows, :]
            return carry

        lax.fori_loop(0, 8, body, 0)

    def remote(src, dst, send, recv, device):
        return pltpu.make_async_remote_copy(
            src_ref=src, dst_ref=dst, send_sem=send, recv_sem=recv, device_id=device, device_id_type=MESH)

    def rs_copy(f, src, dst, j):
        return (
            remote(rs_src.at[f, src], rs_dst.at[f, dst], rs_ss.at[f], rs_rs.at[f], (s, j)),
            remote(rs_src_sc.at[f, src], rs_dst_sc.at[f, dst], rs_ss2.at[f], rs_rs2.at[f], (s, j)),
        )

    def ag_copy(f, src, dst, j):
        return (
            remote(ag_src.at[f, src], ag_dst.at[f, dst], ag_ss.at[f], ag_rs.at[f], (s, j)),
            remote(ag_src_sc.at[f, src], ag_dst_sc.at[f, dst], ag_ss2.at[f], ag_rs2.at[f], (s, j)),
        )

    def all_of(make, f):
        most = pl.ds(0, n_dev - 1)
        return make(f, most, most, peer(1))

    def ag_send(f):
        rows = slice(f * 32, f * 32 + 32)
        code, scale = quantize(own[rows, :])
        ag_src[f, 0] = code
        ag_src_sc[f, 0] = scale
        for k in far_first:
            for copy in ag_copy(f, 0, d, peer(k)):
                copy.start()
        ag_dst[f, d] = code
        ag_dst_sc[f, d] = scale

    def ag_drain(f):
        for copy in all_of(ag_copy, f):
            copy.wait_send()

    def ag_take(f):
        for copy in all_of(ag_copy, f):
            copy.wait_recv()
        for j in range(n_dev):
            hi, low = split(decode(ag_dst[f, j], ag_dst_sc[f, j]))
            rows = slice(f * 512 + j * 32, f * 512 + j * 32 + 32)
            u3[rows, 0:128] = hi
            u3[rows, 128:256] = low
            u3[rows, 256:384] = hi

    def phase1(f):
        rows = slice(f * 512, f * 512 + 512)
        for c in range(4):
            cols = slice(c * 256, (c + 1) * 256)
            err = dm[rows, cols] * mm(u3[rows, :], h3[:, cols], NN) - dr[rows, cols]
            hi, low = split(err)
            e_hi[rows, cols] = hi
            e_lo[rows, cols] = low
        both = mm(e_hi[rows, :], hcat[...], NN)
        grad = both[:, 0:128] + both[:, 128:256] + mm(e_lo[rows, :], hcat[:, 0:128], NN)
        g_tile[...] = grad
        for j in range(n_dev):
            code, scale = quantize(grad[j * 32:j * 32 + 32, :])
            rs_src[f, j] = code
            rs_src_sc[f, j] = scale
        for k in far_first:
            for copy in rs_copy(f, peer(k), d, peer(k)):
                copy.start()
        g_own[f] = g_tile[pl.ds(pl.multiple_of(d * 32, 32), 32), :]

    def rs_sum(f):
        for copy in all_of(rs_copy, f):
            copy.wait_recv()
        total = g_own[f]
        for j in range(n_dev):
            total = total + decode(rs_dst[f, j], rs_dst_sc[f, j])
        rows = slice(f * 32, f * 32 + 32)
        own[rows, :] = SHRINK * own[rows, :] - LEARN_RATE * total

    def rs_drain(f):
        for copy in all_of(rs_copy, f):
            copy.wait_send()

    def h_copy(t, part):
        return (
            remote(h_src.at[part], h_dst.at[t, part], h_ss.at[t], h_rs.at[t], (ahead, d)),
            remote(h_src_sc.at[part], h_dst_sc.at[t, part], h_ss2.at[t], h_rs2.at[t], (ahead, d)),
        )

    def phase2(t):
        def body(c, carry):
            cols = pl.ds(pl.multiple_of(c * 128, 128), 128)
            both = mm(e_hi[:, cols], u3[:, 0:256], TN)
            grad = both[:, 0:128] + both[:, 128:256] + mm(e_lo[:, cols], u3[:, 0:128], TN)
            code, scale = quantize(SHRINK * hcur[cols, :] - LEARN_RATE * grad)
            h_src[c] = code
            h_src_sc[c] = scale
            for copy in h_copy(t, c):
                copy.start()
            return carry

        lax.fori_loop(0, 8, body, 0)

    load(0)
    own[...] = own_ref[...]
    pl.semaphore_wait(barrier, n_dev + 1)
    for f in range(2):
        ag_send(f)
    psm[0] = jnp.zeros_like(psm[0])
    psr[0] = jnp.zeros_like(psr[0])
    for f in range(2):
        rs_dst[f, d] = jnp.zeros((32, 128), I16)
        rs_dst_sc[f, d] = jnp.zeros((1, 128), F32)
    set_h(lambda c, rows: h0_ref[rows, :], True)
    prefix(0)
    load(1)
    dense(0)
    ag_take(0)

    def stratum(t, carry):
        more = t + 1 < STRATA
        phase1(0)
        ag_take(1)
        phase1(1)
        phase2(t)
        rs_sum(0)
        ag_drain(0)

        @pl.when(more)
        def _():
            ag_send(0)
            prefix(t + 1)

        rs_sum(1)
        ag_drain(1)

        @pl.when(more)
        def _():
            ag_send(1)
            dense(t + 1)

        @pl.when(t + 2 < STRATA)
        def _():
            load(t + 2)

        for f in range(2):
            rs_drain(f)
        for copy in h_copy(t, pl.ds(0, 8)):
            copy.wait()

        @pl.when(more)
        def _():
            set_h(lambda c, rows: decode(h_dst[t, c], h_dst_sc[t, c]), True)
            ag_take(0)

        return carry

    lax.fori_loop(0, STRATA, stratum, 0)
    uout_ref[...] = own[...]
    code_ref[...] = h_dst[STRATA - 1]
    scale_ref[...] = h_dst_sc[STRATA - 1]


def finish(own_ref, code_ref, scale_ref, uout_ref, hout_ref):
    uout_ref[...] = own_ref[...]
    for c in range(8):
        hout_ref[c * 128:(c + 1) * 128, :] = decode(code_ref[c], scale_ref[c])


def tile_lists(tile_rows, tile_cols, tile_count):
    slots = tile_rows.shape[1]
    index = jnp.arange(slots, dtype=jnp.int32)
    key = jnp.where(index[None, :] < tile_count, tile_rows * 8 + tile_cols, 64)
    unique = key * slots + index[None, :]
    rank = jnp.sum((unique[:, None, :] < unique[:, :, None]).astype(jnp.int32), axis=2)
    order = jnp.sum(jnp.where(rank[:, None, :] == index[None, :, None], index[None, None, :], 0), axis=2)
    cells = jnp.arange(72, dtype=jnp.int32)
    start = jnp.sum((key[:, None, :] < cells[None, :, None]).astype(jnp.int32), axis=2)
    return order, start


def shards(n_stripe, n_dev, row_factors, col_factors, ratings, rating_mask, tile_rows, tile_cols, tile_count):
    order, start = tile_lists(tile_rows, tile_cols, tile_count)
    vmem, smem, anywhere = (pl.BlockSpec(memory_space=m) for m in (pltpu.VMEM, pltpu.SMEM, pl.ANY))
    dma = lambda n: pltpu.SemaphoreType.DMA((n,))
    own, code, scale = pl.pallas_call(
        functools.partial(kernel, n_stripe, n_dev),
        out_shape=(
            jax.ShapeDtypeStruct(row_factors.shape, F32),
            jax.ShapeDtypeStruct((8, 128, 128), I16),
            jax.ShapeDtypeStruct((8, 1, 128), F32),
        ),
        in_specs=[smem, smem, vmem, vmem, anywhere, anywhere],
        out_specs=(vmem, vmem, vmem),
        scratch_shapes=[
            pltpu.VMEM((32, 128, 128), BF16),
            pltpu.VMEM((32, 128, 128), jnp.int32),
            *[pltpu.VMEM((33, 128, 128), F32)] * 2,
            *[pltpu.VMEM((1024, 1024), F32)] * 2,
            pltpu.VMEM((1024, 384), BF16),
            pltpu.VMEM((384, 1024), BF16),
            pltpu.VMEM((1024, 256), BF16),
            *[pltpu.VMEM((1024, 1024), BF16)] * 2,
            pltpu.VMEM((1024, 128), F32),
            pltpu.VMEM((64, 128), F32),
            pltpu.VMEM((512, 128), F32),
            pltpu.VMEM((2, 32, 128), F32),
            *[pltpu.VMEM((2, 16, 32, 128), I16), pltpu.VMEM((2, 16, 1, 128), F32)] * 2,
            pltpu.VMEM((2, 15, 32, 128), I16),
            pltpu.VMEM((2, 15, 1, 128), F32),
            pltpu.VMEM((2, 16, 32, 128), I16),
            pltpu.VMEM((2, 16, 1, 128), F32),
            pltpu.VMEM((8, 128, 128), I16),
            pltpu.VMEM((8, 1, 128), F32),
            pltpu.VMEM((3, 8, 128, 128), I16),
            pltpu.VMEM((3, 8, 1, 128), F32),
            *[dma(2)] * 9,
            *[dma(3)] * 4,
        ],
        compiler_params=pltpu.CompilerParams(
            collective_id=0, has_side_effects=True, vmem_limit_bytes=56 * 1024 * 1024
        ),
    )(order, start, row_factors, col_factors, ratings, rating_mask)
    return pl.pallas_call(
        finish,
        out_shape=(
            jax.ShapeDtypeStruct(row_factors.shape, F32),
            jax.ShapeDtypeStruct(col_factors.shape, F32),
        ),
        in_specs=[vmem] * 3,
        out_specs=(vmem, vmem),
        compiler_params=pltpu.CompilerParams(vmem_limit_bytes=16 * 1024 * 1024),
    )(own, code, scale)


def solution(mesh):
    in_specs = (
        P(("stripe", "dev"), None),
        P(("stripe", "dev"), None),
        P(None, ("stripe", "dev"), None, None),
        P(None, ("stripe", "dev"), None, None),
        P(None, ("stripe", "dev")),
        P(None, ("stripe", "dev")),
        P(None, ("stripe", "dev")),
    )
    out_specs = (P(("stripe", "dev"), None), P(("stripe", "dev"), None))
    body = functools.partial(shards, mesh.shape["stripe"], mesh.shape["dev"])
    return jax.shard_map(body, mesh=mesh, in_specs=in_specs, out_specs=out_specs, check_vma=False)
```

time: 408 us -> 61.8 us (0.15)
  the two profiles are of different devices: /device:TPU:8 before, /device:TPU:1 now
where the time goes in v2:
time: 61.8 us; the launch traced here: 61.5 us
  Pallas kernels  56.1 us (91%)
  other arithmetic  2.4 us (4%)
  local copies, waits for them, and re-layouts  2.38 us (4%)
  between operations  0.65 us (1%)
    pallas_call x1, Pallas kernels, shards(): pl.pallas_call(functools.partial(kernel, n_stripe, n_dev), out_shape=(jax...  55.3 us
    unnamed x6, local copies, waits for them, and re-layouts  2.38 us

profile of v2, /device:TPU:1, one launch (start us, length us, event | category | flops | bytes accessed | tf_op | source)
XLA Modules:
  0.0 61.5 jit_solution(835274048655302585)
XLA Ops:
  0.6 0.8 %iota_add_fusion = (s32[3,32]{1,0:T(4,128)S(1)}, s32[3,32]{1,0:T(4,128)S(1)}) fusion(s32[3,32]{1,0:T(4,128)} %param.12, s32[3,32]{1,0:T(4,128)} %param.11, s32[3]{0:T(128)} %bitcast.1), kind=kLoop, calls=%fused_computation.5 | loop fusion | flops 576 | bytes 1548 | tf_op jit(solution)/shard_map/add | solution.py:286
  1.4 0.2 convert_reduce_fusion.1
  1.6 0.7 %select_reduce_fusion.order_s = s32[3,32]{1,0:T(4,128)} fusion(s32[3,32]{1,0:T(4,128)S(1)} %convert_reduce_fusion.1), kind=kLoop, calls=%fused_computation.2 | loop fusion | flops 9120 | bytes 768 | tf_op jit(solution)/shard_map/reduce_sum | solution.py:288
  2.4 0.7 %convert_reduce_fusion.start_s = s32[3,72]{1,0:T(4,128)} fusion(s32[3,32]{1,0:T(4,128)S(1)} %get-tuple-element.9), kind=kLoop, calls=%fused_computation | loop fusion | flops 20520 | bytes 1248 | tf_op jit(solution)/shard_map/reduce_sum | solution.py:290
  3.0 55.3 %shard_map.86 = (f32[64,128]{1,0:T(8,128)}, s16[8,128,128]{2,1,0:T(8,128)(2,1)}, f32[8,1,128]{2,1,0:T(1,128)}) custom-call(s32[3,32]{1,0:T(4,128)} %select_reduce_fusion.order_s, s32[3,72]{1,0:T(4,128)} %convert_reduce_fusion.start_s, f32[64,128]{1,0:T(8,128)} %own_ref.1, f32[1024,128]{1,0:T(8,128)} %h0_ref.1, bf16[3,32,128,128]{3,2,1,0:T(8,128)(2,1)} %rat_ref.1, ...), custom_call_target="tpu_custom_call" | custom-call | tf_op jit(solution)/shard_map/pallas_call | solution.py:298
  58.3 0.0 copy-start
  58.3 0.9 %copy-done = s16[8,128,128]{2,1,0:T(8,128)(2,1)S(1)} copy-done((s16[8,128,128]{2,1,0:T(8,128)(2,1)S(1)}, s16[8,128,128]{2,1,0:T(8,128)(2,1)}, u32[]{:S(2)}) %copy-start) | copy-done | bytes 262168
  59.3 0.0 copy-start.1
  59.3 0.8 %copy-done.1 = f32[64,128]{1,0:T(8,128)S(1)} copy-done((f32[64,128]{1,0:T(8,128)S(1)}, f32[64,128]{1,0:T(8,128)}, u32[]{:S(2)}) %copy-start.1) | copy-done | bytes 32792
  60.0 0.0 copy-start.2
  60.0 0.7 %copy-done.2 = f32[8,1,128]{2,1,0:T(1,128)S(1)} copy-done((f32[8,1,128]{2,1,0:T(1,128)S(1)}, f32[8,1,128]{2,1,0:T(1,128)}, u32[]{:S(2)}) %copy-start.2) | copy-done | bytes 4120
  60.7 0.8 %shard_map.87 = (f32[64,128]{1,0:T(8,128)}, f32[1024,128]{1,0:T(8,128)}) custom-call(f32[64,128]{1,0:T(8,128)S(1)} %copy-done.1, s16[8,128,128]{2,1,0:T(8,128)(2,1)S(1)} %copy-done, f32[8,1,128]{2,1,0:T(1,128)S(1)} %copy-done.2), custom_call_target="tpu_custom_call" | custom-call | tf_op jit(solution)/shard_map/pallas_call | solution.py:336
Async XLA Ops:
  58.3 1.0 %copy-start = (s16[8,128,128]{2,1,0:T(8,128)(2,1)S(1)}, s16[8,128,128]{2,1,0:T(8,128)(2,1)}, u32[]{:S(2)}) copy-start(s16[8,128,128]{2,1,0:T(8,128)(2,1)} %get-tuple-element.6.code_ref) | copy-start | bytes 786436
  59.3 0.8 %copy-start.1 = (f32[64,128]{1,0:T(8,128)S(1)}, f32[64,128]{1,0:T(8,128)}, u32[]{:S(2)}) copy-start(f32[64,128]{1,0:T(8,128)} %get-tuple-element.5.own_ref) | copy-start | bytes 98308
  60.0 0.7 %copy-start.2 = (f32[8,1,128]{2,1,0:T(1,128)S(1)}, f32[8,1,128]{2,1,0:T(1,128)}, u32[]{:S(2)}) copy-start(f32[8,1,128]{2,1,0:T(1,128)} %get-tuple-element.7.scale_ref) | copy-start | bytes 12292

commit v3 on v2

--- a/solution.py
+++ b/solution.py
@@ -38,9 +38,26 @@
     return code.astype(jnp.int32).astype(F32) * scale
 
 
+def tile_lists(tile_rows, tile_cols, tile_count, out):
+    slots = tile_rows.shape[1]
+    index = lax.broadcasted_iota(jnp.int32, (STRATA, slots), 1)
+    key = tile_rows[...] * 8 + tile_cols[...]
+    across = lax.broadcasted_iota(jnp.int32, (slots, slots), 1)
+    down = lax.broadcasted_iota(jnp.int32, (slots, slots), 0)
+    place = lax.broadcasted_iota(jnp.int32, (slots, 128), 1)
+    slot = lax.broadcasted_iota(jnp.int32, (slots, 128), 0)
+    for t in range(STRATA):
+        line = jnp.where(index[0:1, :] < tile_count[t], key[t:t + 1, :], 64) * slots + index[0:1, :]
+        line = jnp.broadcast_to(line, (slots, slots))
+        column = jnp.sum(jnp.where(across == down, line, 0), axis=1, keepdims=True)
+        rank = jnp.sum(jnp.where(line < column, 1, 0), axis=1, keepdims=True)
+        out[t:t + 1, :] = jnp.sum(jnp.where(rank == place, slot, 0), axis=0, keepdims=True)
+        out[4 + t:5 + t, :] = jnp.sum(jnp.where(column < place * slots, 1, 0), axis=0, keepdims=True)
+
+
 def kernel(
-    n_stripe, n_dev, order_s, start_s, own_ref, h0_ref, rat_ref, mask_ref, uout_ref, code_ref, scale_ref,
-    rat_v, mask_v, psm, psr, dm, dr, u3, h3, hcat, e_hi, e_lo, hcur, own, g_tile, g_own,
+    n_stripe, n_dev, tr_ref, tc_ref, count_ref, own_ref, h0_ref, rat_ref, mask_ref, uout_ref, code_ref, scale_ref,
+    list_v, list_s, rat_v, mask_v, psm, psr, dm, dr, u3, h3, hcat, e_hi, e_lo, hcur, own, g_tile, g_own,
     rs_src, rs_src_sc, rs_dst, rs_dst_sc, ag_src, ag_src_sc, ag_dst, ag_dst_sc, h_src, h_src_sc, h_dst, h_dst_sc,
     in_sem, rs_ss, rs_rs, rs_ss2, rs_rs2, ag_ss, ag_rs, ag_ss2, ag_rs2, h_ss, h_rs, h_ss2, h_rs2,
 ):
@@ -90,7 +107,7 @@
             copy.wait()
 
         def body(i, carry):
-            slot = order_s[t, i]
+            slot = list_s[t, i]
             seen = mask_v[slot] > 0
             value = jnp.where(seen, rat_v[slot].astype(F32), 0.0)
             psm[i + 1] = psm[i] + jnp.where(seen, 1.0, 0.0)
@@ -102,7 +119,7 @@
     def dense(t):
         def body(r, carry):
             for c in range(8):
-                begin, end = start_s[t, r * 8 + c], start_s[t, r * 8 + c + 1]
+                begin, end = list_s[4 + t, r * 8 + c], list_s[4 + t, r * 8 + c + 1]
                 weight = psm[end] - psm[begin]
                 total = psr[end] - psr[begin]
                 for b in range(2):
@@ -218,12 +235,16 @@
     pl.semaphore_wait(barrier, n_dev + 1)
     for f in range(2):
         ag_send(f)
+    tile_lists(tr_ref, tc_ref, count_ref, list_v)
+    to_scalars = pltpu.make_async_copy(list_v, list_s, in_sem.at[2])
+    to_scalars.start()
     psm[0] = jnp.zeros_like(psm[0])
     psr[0] = jnp.zeros_like(psr[0])
     for f in range(2):
         rs_dst[f, d] = jnp.zeros((32, 128), I16)
         rs_dst_sc[f, d] = jnp.zeros((1, 128), F32)
     set_h(lambda c, rows: h0_ref[rows, :], True)
+    to_scalars.wait()
     prefix(0)
     load(1)
     dense(0)
@@ -273,26 +294,21 @@
     scale_ref[...] = h_dst_sc[STRATA - 1]
 
 
-def finish(own_ref, code_ref, scale_ref, uout_ref, hout_ref):
-    uout_ref[...] = own_ref[...]
+def finish(own_ref, code_ref, scale_ref, uout_ref, hout_ref, code, scale, sems):
+    copies = (
+        pltpu.make_async_copy(code_ref, code, sems.at[0]),
+        pltpu.make_async_copy(scale_ref, scale, sems.at[1]),
+        pltpu.make_async_copy(own_ref, uout_ref, sems.at[2]),
+    )
+    for copy in copies:
+        copy.start()
+    for copy in copies:
+        copy.wait()
     for c in range(8):
-        hout_ref[c * 128:(c + 1) * 128, :] = decode(code_ref[c], scale_ref[c])
-
-
-def tile_lists(tile_rows, tile_cols, tile_count):
-    slots = tile_rows.shape[1]
-    index = jnp.arange(slots, dtype=jnp.int32)
-    key = jnp.where(index[None, :] < tile_count, tile_rows * 8 + tile_cols, 64)
-    unique = key * slots + index[None, :]
-    rank = jnp.sum((unique[:, None, :] < unique[:, :, None]).astype(jnp.int32), axis=2)
-    order = jnp.sum(jnp.where(rank[:, None, :] == index[None, :, None], index[None, None, :], 0), axis=2)
-    cells = jnp.arange(72, dtype=jnp.int32)
-    start = jnp.sum((key[:, None, :] < cells[None, :, None]).astype(jnp.int32), axis=2)
-    return order, start
+        hout_ref[c * 128:(c + 1) * 128, :] = decode(code[c], scale[c])
 
 
 def shards(n_stripe, n_dev, row_factors, col_factors, ratings, rating_mask, tile_rows, tile_cols, tile_count):
-    order, start = tile_lists(tile_rows, tile_cols, tile_count)
     vmem, smem, anywhere = (pl.BlockSpec(memory_space=m) for m in (pltpu.VMEM, pltpu.SMEM, pl.ANY))
     dma = lambda n: pltpu.SemaphoreType.DMA((n,))
     own, code, scale = pl.pallas_call(
@@ -302,9 +318,11 @@
             jax.ShapeDtypeStruct((8, 128, 128), I16),
             jax.ShapeDtypeStruct((8, 1, 128), F32),
         ),
-        in_specs=[smem, smem, vmem, vmem, anywhere, anywhere],
+        in_specs=[vmem, vmem, smem, vmem, vmem, anywhere, anywhere],
         out_specs=(vmem, vmem, vmem),
         scratch_shapes=[
+            pltpu.VMEM((8, 128), jnp.int32),
+            pltpu.SMEM((8, 128), jnp.int32),
             pltpu.VMEM((32, 128, 128), BF16),
             pltpu.VMEM((32, 128, 128), jnp.int32),
             *[pltpu.VMEM((33, 128, 128), F32)] * 2,
@@ -326,22 +344,24 @@
             pltpu.VMEM((8, 1, 128), F32),
             pltpu.VMEM((3, 8, 128, 128), I16),
             pltpu.VMEM((3, 8, 1, 128), F32),
-            *[dma(2)] * 9,
+            dma(3),
+            *[dma(2)] * 8,
             *[dma(3)] * 4,
         ],
         compiler_params=pltpu.CompilerParams(
             collective_id=0, has_side_effects=True, vmem_limit_bytes=56 * 1024 * 1024
         ),
-    )(order, start, row_factors, col_factors, ratings, rating_mask)
+    )(tile_rows, tile_cols, tile_count.reshape(STRATA), row_factors, col_factors, ratings, rating_mask)
     return pl.pallas_call(
         finish,
         out_shape=(
             jax.ShapeDtypeStruct(row_factors.shape, F32),
             jax.ShapeDtypeStruct(col_factors.shape, F32),
         ),
-        in_specs=[vmem] * 3,
+        in_specs=[anywhere] * 3,
         out_specs=(vmem, vmem),
-        compiler_params=pltpu.CompilerParams(vmem_limit_bytes=16 * 1024 * 1024),
+        scratch_shapes=[pltpu.VMEM((8, 128, 128), I16), pltpu.VMEM((8, 1, 128), F32), dma(3)],
+        compiler_params=pltpu.CompilerParams(vmem_limit_bytes=63400000),
     )(own, code, scale)
 
 

time: 61.8 us -> 57.8 us (0.935)
  the two profiles are of different devices: /device:TPU:1 before, /device:TPU:8 now
where the time goes in v3:
time: 57.8 us; the launch traced here: 57.5 us
  Pallas kernels  56.8 us (98%)
  between operations  0.64 us (1%)
    pallas_call x1, Pallas kernels, shards(): pl.pallas_call(functools.partial(kernel, n_stripe, n_dev), out_shape=(jax...  55 us
    pallas_call x1, Pallas kernels, shards(): pl.pallas_call(finish, out_shape=(jax.ShapeDtypeStruct(row_factors.shape,...  1.83 us

profile of v3, /device:TPU:8, one launch (start us, length us, event | category | flops | bytes accessed | tf_op | source)
XLA Modules:
  0.0 57.5 jit_solution(14341496942223623912)
XLA Ops:
  0.6 55.0 %shard_map.86 = (f32[64,128]{1,0:T(8,128)}, s16[8,128,128]{2,1,0:T(8,128)(2,1)}, f32[8,1,128]{2,1,0:T(1,128)}) custom-call(s32[3,32]{1,0:T(4,128)} %tr_ref.1, s32[3,32]{1,0:T(4,128)} %tc_ref.1, s32[3]{0:T(128)} %bitcast.1, f32[64,128]{1,0:T(8,128)} %own_ref.1, f32[1024,128]{1,0:T(8,128)} %h0_ref.1, bf16[3,32,128,128]{3,2,1,0:T(8,128)(2,1)} %rat_ref.1, ...), custom_call_target="tpu_custom_call" | custom-call | tf_op jit(solution)/shard_map/pallas_call | solution.py:314
  55.6 1.8 %shard_map.87 = (f32[64,128]{1,0:T(8,128)}, f32[1024,128]{1,0:T(8,128)}) custom-call(f32[64,128]{1,0:T(8,128)} %get-tuple-element.5.own_ref, s16[8,128,128]{2,1,0:T(8,128)(2,1)} %get-tuple-element.6.code_ref, f32[8,1,128]{2,1,0:T(1,128)} %get-tuple-element.7.scale_ref), custom_call_target="tpu_custom_call" | custom-call | tf_op jit(solution)/shard_map/pallas_call | solution.py:355

commit v4 on v3

--- a/solution.py
+++ b/solution.py
@@ -9,6 +9,7 @@
 
 MESH = pl.DeviceIdType.MESH
 STRATA = 3
+PARTS = 4
 LEARN_RATE = 0.02
 RIDGE_WEIGHT = 2.5
 SHRINK = 1.0 - LEARN_RATE * RIDGE_WEIGHT
@@ -123,9 +124,9 @@
                 weight = psm[end] - psm[begin]
                 total = psr[end] - psr[begin]
                 for b in range(2):
-                    for f in range(2):
-                        rows = slice(b * 64 + f * 32, b * 64 + f * 32 + 32)
-                        at = pl.ds(pl.multiple_of(f * 512 + r * 64 + b * 32, 32), 32)
+                    for f in range(PARTS):
+                        rows = slice(b * 64 + f * 16, b * 64 + f * 16 + 16)
+                        at = pl.ds(pl.multiple_of(f * 256 + r * 32 + b * 16, 16), 16)
                         dm[at, c * 128:(c + 1) * 128] = weight[rows, :]
                         dr[at, c * 128:(c + 1) * 128] = total[rows, :]
             return carry
@@ -153,7 +154,7 @@
         return make(f, most, most, peer(1))
 
     def ag_send(f):
-        rows = slice(f * 32, f * 32 + 32)
+        rows = slice(f * 16, f * 16 + 16)
         code, scale = quantize(own[rows, :])
         ag_src[f, 0] = code
         ag_src_sc[f, 0] = scale
@@ -172,13 +173,13 @@
             copy.wait_recv()
         for j in range(n_dev):
             hi, low = split(decode(ag_dst[f, j], ag_dst_sc[f, j]))
-            rows = slice(f * 512 + j * 32, f * 512 + j * 32 + 32)
+            rows = slice(f * 256 + j * 16, f * 256 + j * 16 + 16)
             u3[rows, 0:128] = hi
             u3[rows, 128:256] = low
             u3[rows, 256:384] = hi
 
     def phase1(f):
-        rows = slice(f * 512, f * 512 + 512)
+        rows = slice(f * 256, f * 256 + 256)
         for c in range(4):
             cols = slice(c * 256, (c + 1) * 256)
             err = dm[rows, cols] * mm(u3[rows, :], h3[:, cols], NN) - dr[rows, cols]
@@ -189,13 +190,13 @@
         grad = both[:, 0:128] + both[:, 128:256] + mm(e_lo[rows, :], hcat[:, 0:128], NN)
         g_tile[...] = grad
         for j in range(n_dev):
-            code, scale = quantize(grad[j * 32:j * 32 + 32, :])
+            code, scale = quantize(grad[j * 16:j * 16 + 16, :])
             rs_src[f, j] = code
             rs_src_sc[f, j] = scale
         for k in far_first:
             for copy in rs_copy(f, peer(k), d, peer(k)):
                 copy.start()
-        g_own[f] = g_tile[pl.ds(pl.multiple_of(d * 32, 32), 32), :]
+        g_own[f] = g_tile[pl.ds(pl.multiple_of(d * 16, 16), 16), :]
 
     def rs_sum(f):
         for copy in all_of(rs_copy, f):
@@ -203,7 +204,7 @@
         total = g_own[f]
         for j in range(n_dev):
             total = total + decode(rs_dst[f, j], rs_dst_sc[f, j])
-        rows = slice(f * 32, f * 32 + 32)
+        rows = slice(f * 16, f * 16 + 16)
         own[rows, :] = SHRINK * own[rows, :] - LEARN_RATE * total
 
     def rs_drain(f):
@@ -211,10 +212,16 @@
             copy.wait_send()
 
     def h_copy(t, part):
+        sem = 8 * t + part
         return (
-            remote(h_src.at[part], h_dst.at[t, part], h_ss.at[t], h_rs.at[t], (ahead, d)),
-            remote(h_src_sc.at[part], h_dst_sc.at[t, part], h_ss2.at[t], h_rs2.at[t], (ahead, d)),
+            remote(h_src.at[part], h_dst.at[t, part], h_ss.at[sem], h_rs.at[sem], (ahead, d)),
+            remote(h_src_sc.at[part], h_dst_sc.at[t, part], h_ss2.at[sem], h_rs2.at[sem], (ahead, d)),
         )
+
+    def h_landed(t, part):
+        for copy in h_copy(t, part):
+            copy.wait_recv()
+        return decode(h_dst[t, part], h_dst_sc[t, part])
 
     def phase2(t):
         def body(c, carry):
@@ -233,15 +240,15 @@
     load(0)
     own[...] = own_ref[...]
     pl.semaphore_wait(barrier, n_dev + 1)
-    for f in range(2):
+    for f in range(PARTS):
         ag_send(f)
     tile_lists(tr_ref, tc_ref, count_ref, list_v)
     to_scalars = pltpu.make_async_copy(list_v, list_s, in_sem.at[2])
     to_scalars.start()
     psm[0] = jnp.zeros_like(psm[0])
     psr[0] = jnp.zeros_like(psr[0])
-    for f in range(2):
-        rs_dst[f, d] = jnp.zeros((32, 128), I16)
+    for f in range(PARTS):
+        rs_dst[f, d] = jnp.zeros((16, 128), I16)
         rs_dst_sc[f, d] = jnp.zeros((1, 128), F32)
     set_h(lambda c, rows: h0_ref[rows, :], True)
     to_scalars.wait()
@@ -253,45 +260,51 @@
     def stratum(t, carry):
         more = t + 1 < STRATA
         phase1(0)
-        ag_take(1)
-        phase1(1)
+        for f in range(1, PARTS):
+            ag_take(f)
+            phase1(f)
         phase2(t)
-        rs_sum(0)
-        ag_drain(0)
+        for f in range(PARTS):
+            rs_sum(f)
+            ag_drain(f)
+
+            @pl.when(more)
+            def _():
+                ag_send(f)
+
 
         @pl.when(more)
         def _():
-            ag_send(0)
             prefix(t + 1)
-
-        rs_sum(1)
-        ag_drain(1)
-
-        @pl.when(more)
-        def _():
-            ag_send(1)
             dense(t + 1)
 
         @pl.when(t + 2 < STRATA)
         def _():
             load(t + 2)
 
-        for f in range(2):
+        for f in range(PARTS):
             rs_drain(f)
-        for copy in h_copy(t, pl.ds(0, 8)):
-            copy.wait()
-
         @pl.when(more)
         def _():
-            set_h(lambda c, rows: decode(h_dst[t, c], h_dst_sc[t, c]), True)
+            set_h(lambda c, rows: h_landed(t, c), True)
             ag_take(0)
+
+        def sent(c, carry):
+            for copy in h_copy(t, c):
+                copy.wait_send()
+            return carry
+
+        lax.fori_loop(0, 8, sent, 0)
 
         return carry
 
     lax.fori_loop(0, STRATA, stratum, 0)
     uout_ref[...] = own[...]
-    code_ref[...] = h_dst[STRATA - 1]
-    scale_ref[...] = h_dst_sc[STRATA - 1]
+    for c in range(8):
+        for copy in h_copy(STRATA - 1, c):
+            copy.wait_recv()
+        code_ref[c] = h_dst[STRATA - 1, c]
+        scale_ref[c] = h_dst_sc[STRATA - 1, c]
 
 
 def finish(own_ref, code_ref, scale_ref, uout_ref, hout_ref, code, scale, sems):
@@ -333,20 +346,20 @@
             *[pltpu.VMEM((1024, 1024), BF16)] * 2,
             pltpu.VMEM((1024, 128), F32),
             pltpu.VMEM((64, 128), F32),
-            pltpu.VMEM((512, 128), F32),
-            pltpu.VMEM((2, 32, 128), F32),
-            *[pltpu.VMEM((2, 16, 32, 128), I16), pltpu.VMEM((2, 16, 1, 128), F32)] * 2,
-            pltpu.VMEM((2, 15, 32, 128), I16),
-            pltpu.VMEM((2, 15, 1, 128), F32),
-            pltpu.VMEM((2, 16, 32, 128), I16),
-            pltpu.VMEM((2, 16, 1, 128), F32),
+            pltpu.VMEM((256, 128), F32),
+            pltpu.VMEM((PARTS, 16, 128), F32),
+            *[pltpu.VMEM((PARTS, 16, 16, 128), I16), pltpu.VMEM((PARTS, 16, 1, 128), F32)] * 2,
+            pltpu.VMEM((PARTS, 15, 16, 128), I16),
+            pltpu.VMEM((PARTS, 15, 1, 128), F32),
+            pltpu.VMEM((PARTS, 16, 16, 128), I16),
+            pltpu.VMEM((PARTS, 16, 1, 128), F32),
             pltpu.VMEM((8, 128, 128), I16),
             pltpu.VMEM((8, 1, 128), F32),
             pltpu.VMEM((3, 8, 128, 128), I16),
             pltpu.VMEM((3, 8, 1, 128), F32),
             dma(3),
-            *[dma(2)] * 8,
-            *[dma(3)] * 4,
+            *[dma(PARTS)] * 8,
+            *[dma(24)] * 4,
         ],
         compiler_params=pltpu.CompilerParams(
             collective_id=0, has_side_effects=True, vmem_limit_bytes=56 * 1024 * 1024

time: 57.8 us -> 58.5 us (1.012)
  Pallas kernels: 56.8 us -> 57.8 us
    pallas_call x1, Pallas kernels: 55 us -> 55.9 us  [shards(): pl.pallas_call(functools.partial(kernel, n_stripe, n_dev), out_shape=(jax...]
where the time goes in v4:
time: 58.5 us; the launch traced here: 58.4 us
  Pallas kernels  57.8 us (99%)
  between operations  0.64 us (1%)
    pallas_call x1, Pallas kernels, shards(): pl.pallas_call(functools.partial(kernel, n_stripe, n_dev), out_shape=(jax...  55.9 us
    pallas_call x1, Pallas kernels, shards(): pl.pallas_call(finish, out_shape=(jax.ShapeDtypeStruct(row_factors.shape,...  1.83 us

profile of v4, /device:TPU:8, one launch (start us, length us, event | category | flops | bytes accessed | tf_op | source)
XLA Modules:
  0.0 58.4 jit_solution(18374190284671518942)
XLA Ops:
  0.6 55.9 %shard_map.86 = (f32[64,128]{1,0:T(8,128)}, s16[8,128,128]{2,1,0:T(8,128)(2,1)}, f32[8,1,128]{2,1,0:T(1,128)}) custom-call(s32[3,32]{1,0:T(4,128)} %tr_ref.1, s32[3,32]{1,0:T(4,128)} %tc_ref.1, s32[3]{0:T(128)} %bitcast.1, f32[64,128]{1,0:T(8,128)} %own_ref.1, f32[1024,128]{1,0:T(8,128)} %h0_ref.1, bf16[3,32,128,128]{3,2,1,0:T(8,128)(2,1)} %rat_ref.1, ...), custom_call_target="tpu_custom_call" | custom-call | tf_op jit(solution)/shard_map/pallas_call | solution.py:327
  56.6 1.8 %shard_map.87 = (f32[64,128]{1,0:T(8,128)}, f32[1024,128]{1,0:T(8,128)}) custom-call(f32[64,128]{1,0:T(8,128)} %get-tuple-element.5.own_ref, s16[8,128,128]{2,1,0:T(8,128)(2,1)} %get-tuple-element.6.code_ref, f32[8,1,128]{2,1,0:T(1,128)} %get-tuple-element.7.scale_ref), custom_call_target="tpu_custom_call" | custom-call | tf_op jit(solution)/shard_map/pallas_call | solution.py:368
